TPU v7x, 256 devices: a whole 4x4x8 slice. The times are simulated.
256 devices in a mesh: doc: 32 (over z_lo, x, core), term: 8 (over y, z_hi).
Axes of the slice: x: 4, y: 4, z: 8 (z_hi: 2, z_lo: 4; z = z_hi * 4 + z_lo), core: 2. Of those that a mesh axis runs over, the one named last changes fastest.
Arguments:
- blocks: bfloat16 [32, 2560, 128, 128], P('doc', 'term'), may hold values from -6 to 6
- block_rows: int32 [32, 2560], P('doc', 'term'), may hold values from 0 to 63, as said below
- block_cols: int32 [32, 2560], P('doc', 'term'), may hold values from 0 to 63, as said below
- counts: int32 [32, 8], P('doc', 'term'), may hold values from 80 to 320, as said below
- start_panel: float32 [16, 65536], P(None, 'term'), may hold values from -6 to 6
Outputs:
- left_panel: float32 [16, 262144], P(None, 'doc')
- right_panel: float32 [16, 65536], P(None, 'term')
Inputs may be any that keep to these rules, and one draw needn't show every extreme that they name: `block_rows`: within one tile the slots name distinct blocks. `block_cols`: within one tile the slots name distinct blocks. Some tile uses all 320 slots; slots from counts on are unused.
All inputs are finite; a program needn't handle non-finite values.
Results may differ from a plain program's by a relative error of at most 0.0092.
Values sent between devices are 32-bit elements; how exact they have to be, the bound alone decides.
No kernel may reach another device: no remote copies, remote signals or barrier semaphores. Data moves between devices by JAX's collectives and lax.ppermute only.
A program may use at most 64 MiB of HBM per device.

v0:
```python
import jax
import jax.numpy as jnp
from jax import lax
from jax.sharding import PartitionSpec as P

BLK = 128
BR = 64
BC = 64
ITERS = 2


def slot_product(tile_blocks, source_slots, target_slots, live, panel_bf, target_count, forward):
    block_width = panel_bf.shape[0]
    block_size = tile_blocks.shape[-1]
    pieces = panel_bf.reshape(block_width, -1, block_size)
    gathered = jnp.take(pieces, source_slots, axis=1)
    pattern = "nrc,knc->knr" if forward else "nrc,knr->knc"
    products = jnp.einsum(pattern, tile_blocks, gathered, preferred_element_type=jnp.float32)
    targets = jnp.arange(target_count, dtype=jnp.int32)
    onehot = jnp.where(
        live[:, None] & (target_slots[:, None] == targets[None, :]), 1.0, 0.0
    ).astype(jnp.float32)
    return jnp.einsum("knr,nb->kbr", products, onehot, precision=lax.Precision.HIGHEST)


def orthonormal(block_in, prior, count_all, reducer):
    hp = lax.Precision.HIGHEST
    if prior is None:
        gram = reducer(jnp.dot(block_in, block_in.T, precision=hp)) / count_all
        projected = block_in
    else:
        coeffs = reducer(jnp.dot(block_in, prior.T, precision=hp)) / count_all
        projected = block_in - jnp.dot(coeffs, prior, precision=hp)
        gram = reducer(jnp.dot(projected, projected.T, precision=hp)) / count_all
    factor = jnp.linalg.cholesky(gram)
    return lax.linalg.triangular_solve(factor, projected, left_side=True, lower=True)


def start_reduce(values):
    return lax.psum(values, "term")


def left_reduce(values):
    return lax.psum(values, "doc")


def right_reduce(values):
    return lax.psum(values, "term")


def local(blocks, block_rows, block_cols, counts, start_panel):
    tile_blocks = blocks[0]
    row_slots = block_rows[0]
    column_slots = block_cols[0]
    live_count = counts[0, 0]
    slot_total = tile_blocks.shape[0]
    docs_all = BR * BLK * lax.axis_size("doc")
    terms_all = BC * BLK * lax.axis_size("term")

    def multiply(panel_bf, source_slots, target_slots, target_count, forward):
        live = jnp.arange(slot_total, dtype=jnp.int32) < live_count
        summed = slot_product(
            tile_blocks, source_slots, target_slots, live, panel_bf, target_count, forward
        )
        return summed.reshape(panel_bf.shape[0], target_count * tile_blocks.shape[-1])

    right_panel = orthonormal(start_panel, None, terms_all, start_reduce)
    left_panel = None
    for sweep in range(ITERS):
        partial_left = multiply(right_panel.astype(jnp.bfloat16), column_slots, row_slots, BR, True)
        summed_left = lax.psum(partial_left, "term")
        left_panel = orthonormal(summed_left, left_panel, docs_all, left_reduce)
        partial_right = multiply(
            left_panel.astype(jnp.bfloat16), row_slots, column_slots, BC, False
        )
        summed_right = lax.psum(partial_right, "doc")
        right_panel = orthonormal(summed_right, right_panel, terms_all, right_reduce)
    return (left_panel, right_panel)


def solution(mesh):
    return jax.shard_map(
        local,
        mesh=mesh,
        in_specs=(
            P("doc", "term", None, None),
            P("doc", "term"),
            P("doc", "term"),
            P("doc", "term"),
            P(None, "term"),
        ),
        out_specs=(P(None, "doc"), P(None, "term")),
        check_vma=False,
    )
```

profile of v0, /device:TPU:1, one launch (start us, length us, event | category | flops | bytes accessed | tf_op | source)
XLA Modules:
  0.0 1201.8 jit_solution(5936789600723642730)
XLA Ops:
  7.2 0.7 reduce.5
  8.7 0.7 reduce.4
  9.4 0.8 fusion.113
  10.2 31.0 %psum.84 = f32[16,16]{0,1:T(8,128)S(1)} all-reduce(f32[16,16]{0,1:T(8,128)S(1)} %fusion.113), channel_id=1, replica_groups=mesh['doc'=32,'term'=8] {'term'}, use_global_device_ids=true, to_apply=%region_0.0 | all-reduce | flops 256 | bytes 2048 | tf_op jit(solution)/shard_map/psum | solution.py:40
  41.3 1.5 cholesky.89
  42.7 0.6 compare_reduce_fusion.4
  43.4 0.6 fusion.66
  44.0 1.2 custom-call.9
  46.0 1.9 gather_fusion
  47.8 8.3 fusion.6
  56.1 2.6 fusion.14
  58.7 1.1 copy.75
  59.9 107.2 %all-reduce.5.cloned.1.call-done = f32[16,8192]{1,0:T(8,128)} async-done(((f32[16,8192]{1,0:T(8,128)}), f32[16,8192]{1,0:T(8,128)}) %all-reduce.5.cloned.1.call-update) | async-done | bytes 524304 | tf_op jit(solution)/shard_map/psum | solution.py:71
  167.1 2.0 fusion.114
  169.1 71.7 %psum.86 = f32[16,16]{0,1:T(8,128)S(1)} all-reduce(f32[16,16]{0,1:T(8,128)S(1)} %fusion.114), channel_id=1, replica_groups=mesh['doc'=32,'term'=8] {'doc'}, use_global_device_ids=true, to_apply=%region_4.8 | all-reduce | flops 256 | bytes 2048 | tf_op jit(solution)/shard_map/psum | solution.py:44
  240.9 1.5 cholesky.100
  242.3 0.6 compare_reduce_fusion.3
  243.0 0.6 fusion.67
  243.6 1.2 custom-call.10
  244.9 1.7 fusion.80
  246.6 1.9 gather_fusion.1
  248.5 5.6 fusion.4
  254.1 2.5 fusion.12
  256.6 1.1 copy.74
  257.8 267.8 %all-reduce.7.cloned.1.call-done = f32[16,8192]{1,0:T(8,128)} async-done(((f32[16,8192]{1,0:T(8,128)}), f32[16,8192]{1,0:T(8,128)}) %all-reduce.7.cloned.1.call-update) | async-done | bytes 524304 | tf_op jit(solution)/shard_map/psum | solution.py:76
  525.6 1.8 fusion.115
  527.4 25.7 %psum.88 = f32[16,16]{0,1:T(8,128)S(1)} all-reduce(f32[16,16]{0,1:T(8,128)S(1)} %fusion.115), channel_id=1, replica_groups=mesh['doc'=32,'term'=8] {'term'}, use_global_device_ids=true, to_apply=%region_6.10 | all-reduce | flops 256 | bytes 2048 | tf_op jit(solution)/shard_map/psum | solution.py:48
  553.2 1.7 convolution_subtract_fusion.2
  554.8 0.8 fusion.116
  555.6 21.6 %psum.89 = f32[16,16]{0,1:T(8,128)S(1)} all-reduce(f32[16,16]{0,1:T(8,128)S(1)} %fusion.116), channel_id=1, replica_groups=mesh['doc'=32,'term'=8] {'term'}, use_global_device_ids=true, to_apply=%region_7.11 | all-reduce | flops 256 | bytes 2048 | tf_op jit(solution)/shard_map/psum | solution.py:48
  577.3 1.5 cholesky.111
  578.8 0.6 compare_reduce_fusion.2
  579.5 0.6 fusion.68
  580.1 1.2 custom-call.11
  581.4 0.6 fusion.77
  582.0 1.9 gather_fusion.2
  583.9 8.3 fusion.2
  592.2 2.6 fusion.10
  594.7 1.1 copy.73
  595.9 114.1 %all-reduce.9.cloned.1.call-done = f32[16,8192]{1,0:T(8,128)} async-done(((f32[16,8192]{1,0:T(8,128)}), f32[16,8192]{1,0:T(8,128)}) %all-reduce.9.cloned.1.call-update) | async-done | bytes 524304 | tf_op jit(solution)/shard_map/psum | solution.py:71
  710.0 1.8 fusion.117
  711.9 71.5 %psum.91 = f32[16,16]{0,1:T(8,128)S(1)} all-reduce(f32[16,16]{0,1:T(8,128)S(1)} %fusion.117), channel_id=1, replica_groups=mesh['doc'=32,'term'=8] {'doc'}, use_global_device_ids=true, to_apply=%region_9.13 | all-reduce | flops 256 | bytes 2048 | tf_op jit(solution)/shard_map/psum | solution.py:44
  783.4 1.7 convolution_subtract_fusion.1
  785.0 0.8 fusion.118
  785.8 68.7 %psum.92 = f32[16,16]{0,1:T(8,128)S(1)} all-reduce(f32[16,16]{0,1:T(8,128)S(1)} %fusion.118), channel_id=1, replica_groups=mesh['doc'=32,'term'=8] {'doc'}, use_global_device_ids=true, to_apply=%region_10.14 | all-reduce | flops 256 | bytes 2048 | tf_op jit(solution)/shard_map/psum | solution.py:44
  854.6 1.5 cholesky.122
  856.1 0.6 compare_reduce_fusion.1
  856.7 0.6 fusion.69
  857.4 1.2 custom-call.12
  859.3 1.9 gather_fusion.3
  861.2 5.6 fusion
  866.8 2.5 fusion.8
  869.4 1.1 copy.72
  870.5 267.8 %all-reduce.11.cloned.1.call-done = f32[16,8192]{1,0:T(8,128)} async-done(((f32[16,8192]{1,0:T(8,128)}), f32[16,8192]{1,0:T(8,128)}) %all-reduce.11.cloned.1.call-update) | async-done | bytes 524304 | tf_op jit(solution)/shard_map/psum | solution.py:76
  1138.3 1.8 fusion.119
  1140.2 25.7 %psum.94 = f32[16,16]{0,1:T(8,128)S(1)} all-reduce(f32[16,16]{0,1:T(8,128)S(1)} %fusion.119), channel_id=1, replica_groups=mesh['doc'=32,'term'=8] {'term'}, use_global_device_ids=true, to_apply=%region_12.16 | all-reduce | flops 256 | bytes 2048 | tf_op jit(solution)/shard_map/psum | solution.py:48
  1165.9 1.7 convolution_subtract_fusion
  1167.6 0.8 fusion.120
  1168.3 21.4 %psum.95 = f32[16,16]{0,1:T(8,128)S(1)} all-reduce(f32[16,16]{0,1:T(8,128)S(1)} %fusion.120), channel_id=1, replica_groups=mesh['doc'=32,'term'=8] {'term'}, use_global_device_ids=true, to_apply=%region_13.17 | all-reduce | flops 256 | bytes 2048 | tf_op jit(solution)/shard_map/psum | solution.py:48
  1189.8 1.5 cholesky.133
  1191.3 0.6 compare_reduce_fusion
  1192.0 0.6 fusion.70
  1192.6 1.2 custom-call.13
  1193.9 1.4 fusion.71
  (45 shorter events, 2.3 us)
Async XLA Ops:
  7.2 2.2 copy-start
  7.2 159.9 %all-reduce.5.cloned.1.call-start = ((), (), s32[]{:S(2)}) async-start(), calls=%async_computation | async-start | bytes 1048576 | tf_op jit(solution)/shard_map/psum | solution.py:71
  59.8 465.8 %all-reduce.7.cloned.1.call-start = ((), (), s32[]{:S(2)}) async-start(), calls=%async_computation.1 | async-start | bytes 1048576 | tf_op jit(solution)/shard_map/psum | solution.py:76
  257.8 452.3 %all-reduce.9.cloned.1.call-start = ((), (), s32[]{:S(2)}) async-start(), calls=%async_computation.2 | async-start | bytes 1048576 | tf_op jit(solution)/shard_map/psum | solution.py:71
  595.9 542.5 %all-reduce.11.cloned.1.call-start = ((), (), s32[]{:S(2)}) async-start(), calls=%async_computation.3 | async-start | bytes 1048576 | tf_op jit(solution)/shard_map/psum | solution.py:76
  859.3 7.5 copy-start.1
Sparse Core Ops, SparseCore 0:
  59.9 107.1 all-reduce.4
  257.9 267.6 all-reduce.6
  596.0 113.9 all-reduce.8
  870.6 267.6 all-reduce.10
where the time goes:
time: 1210 us; the launch traced here: 1200 us
  waiting for transfers between devices  757 us (63%)
  blocking collectives  337 us (28%)
  matrix products  58.6 us (5%)
  other arithmetic  21.7 us (2%)
  between operations  14.8 us (1%)
  local copies, waits for them, and re-layouts  12.2 us (1%)
    psum x2, waiting for transfers between devices, local(): summed_right = lax.psum(partial_right, 'doc')  536 us
    psum x2, waiting for transfers between devices, local(): summed_left = lax.psum(partial_left, 'term')  221 us
    psum x3, blocking collectives, left_reduce(): return lax.psum(values, 'doc')  212 us
    psum x4, blocking collectives, right_reduce(): return lax.psum(values, 'term')  94.4 us
    psum x1, blocking collectives, start_reduce(): return lax.psum(values, 'term')  31 us
    dot_general x4, matrix products, slot_product(): jnp.einsum(pattern, tile_blocks, gathered, preferred_element_type=jnp.flo...  27.7 us
  transfers between devices with their start and end apart: 4, of which 4 were waited for; matrix products, arithmetic and copies ran while one was open for 0% of the time, Pallas kernels for 0%

commit v1 on v0

v1 whole, which is shorter than its diff:
```python
import functools

import jax
import jax.numpy as jnp
import numpy as np
from jax import lax
from jax.experimental import pallas as pl
from jax.experimental.pallas import tpu as pltpu
from jax.sharding import Mesh
from jax.sharding import PartitionSpec as P

BLK = 128
K = 16
BR = 64
NB = 320
CHUNK = 32
UNROLL = 8
DOC = ("zl", "x", "c")
TERM = ("y", "zh")
F32 = jnp.float32
BF = jnp.bfloat16
HI = lax.Precision.HIGHEST
VMEM = pltpu.VMEM
SMEM = pltpu.SMEM


def mm(a, b):
    return jnp.dot(a, b, precision=HI, preferred_element_type=F32)


def mmt(a, b):
    return lax.dot_general(a, b, (((1,), (1,)), ((), ())), precision=HI, preferred_element_type=F32)


def inverse_factor(gram):
    lane = lax.broadcasted_iota(jnp.int32, (K, BLK), 1)
    row = lax.broadcasted_iota(jnp.int32, (K, BLK), 0)
    aug = jnp.concatenate([gram, jnp.zeros((K, BLK - K), F32)], axis=1)
    aug = jnp.where(lane == row + K, 1.0, aug)
    for j in range(K - 1):
        pivot_row = aug[j : j + 1, :]
        ratio = pivot_row / pivot_row[:, j : j + 1]
        aug = aug - jnp.where(row > j, aug[:, j : j + 1], 0.0) * ratio
    diag = jnp.sum(jnp.where(lane == row, aug, 0.0), axis=1, keepdims=True)
    return aug[:, K : 2 * K] * lax.rsqrt(diag)


def columns(matrix):
    return [jnp.broadcast_to(matrix[:, j : j + 1], (K, BLK)) for j in range(K)]


def combine(cols, piece):
    total = cols[0] * piece[0:1, :]
    for j in range(1, K):
        total = total + cols[j] * piece[j : j + 1, :]
    return total


def split_store(split_ref, index, value):
    high = value.astype(BF)
    rest = value - high.astype(F32)
    middle = rest.astype(BF)
    low = (rest - middle.astype(F32)).astype(BF)
    split_ref[index, 0:16, :] = high
    split_ref[index, 16:32, :] = middle
    split_ref[index, 32:48, :] = low


def fold(wide):
    rows = (wide[32:48, :] + wide[16:32, :]) + wide[0:16, :]
    return (rows[:, 32:48] + rows[:, 16:32]) + rows[:, 0:16]


def gram_of(left_ref, right_ref, count=BR):
    def step(i, total):
        return total + lax.dot_general(
            left_ref[i], right_ref[i], (((1,), (1,)), ((), ())), preferred_element_type=F32
        )

    return fold(lax.fori_loop(0, count, step, jnp.zeros((48, 48), F32), unroll=8))


def pad_lanes(*parts):
    width = sum(p.shape[1] for p in parts)
    return jnp.concatenate([*parts, jnp.zeros((K, BLK - width), F32)], axis=1)


def start_copies(blocks_ref, held, sems):
    for i in range(NB // CHUNK):
        part = pl.ds(i * CHUNK, CHUNK)
        pltpu.make_async_copy(blocks_ref.at[0, part], held.at[part], sems.at[i]).start()


def multiply(scal, src_ref, tgt_ref, blocks_ref, held, sems, split, acc, place, spare, forward):
    acc[...] = jnp.zeros_like(acc)
    live = scal[0]
    dims = (((1,), (1,)), ((), ())) if forward else (((1,), (0,)), ((), ()))

    def chunk_step(i, carry):
        part = pl.ds(i * CHUNK, CHUNK)
        pltpu.make_async_copy(blocks_ref.at[0, part], held.at[part], sems.at[i]).wait()
        left = jnp.clip(live - i * CHUNK, 0, CHUNK)
        groups = lax.div(left + (UNROLL - 1), UNROLL)

        def group_step(g, inner):
            base = i * CHUNK + g * UNROLL
            places, values = [], []
            for u in range(UNROLL):
                slot = base + u
                wide = lax.dot_general(
                    split[src_ref[0, slot]], held[slot], dims, preferred_element_type=F32
                )
                values.append((wide[32:48, :] + wide[16:32, :]) + wide[0:16, :])
                places.append(jnp.where(slot < live, place(tgt_ref[0, slot]), spare))
            for where_to, value in zip(places, values):
                acc[where_to] += value
            return inner

        lax.fori_loop(0, groups, group_step, 0)
        return carry

    lax.fori_loop(0, NB // CHUNK, chunk_step, 0)


def term_place(target):
    return lax.shift_right_logical(target, 4) * 17 + jnp.bitwise_and(target, 15)


def doc_place(core):
    def place(target):
        half = jnp.bitwise_xor(lax.shift_right_logical(target, 5), core)
        quarter = jnp.bitwise_and(lax.shift_right_logical(target, 3), 3)
        return half * 36 + quarter * 9 + jnp.bitwise_and(target, 7)

    return place


def first_forward(scal, rows, cols, start, blocks, acc, held, sems, split):
    start_copies(blocks, held, sems)
    for i in range(BR):
        split_store(split, i, start[:, i * BLK : (i + 1) * BLK])
    ext = pad_lanes(gram_of(split, split))
    multiply(scal, cols, rows, blocks, held, sems, split, acc, term_place, 16, True)
    for j in range(4):
        acc[j * 17 + 16] = ext


def first_backward(
    scal, rows, cols, summed, ext, blocks, own, other, left_raw, mr0, held, sems, split, acc, *, terms
):
    start_copies(blocks, held, sems)
    inverse = inverse_factor(ext[:, 0:K] / terms)
    mr0[...] = pad_lanes(inverse)
    cols_m = columns(inverse)

    def step(i, carry):
        value = combine(cols_m, summed[i])
        left_raw[i] = value
        split_store(split, i, value)
        return carry

    lax.fori_loop(0, BR, step, 0, unroll=2)
    out = pad_lanes(gram_of(split, split))
    multiply(scal, rows, cols, blocks, held, sems, split, acc, doc_place(scal[1]), 8, False)
    for j in range(8):
        acc[j * 9 + 8] = out
    own[...] = acc[0:36]
    other[...] = acc[36:72]


def second_forward(
    scal, rows, cols, mine, theirs, ext, start, mr0, blocks, acc, right_raw, right0, ml1,
    held, sems, split, split0, *, docs
):
    start_copies(blocks, held, sems)
    core = scal[1]
    inverse = inverse_factor(ext[:, 0:K] / docs)
    ml1[...] = pad_lanes(inverse)
    cols_m = columns(inverse)

    def half(source, base):
        def step(i, carry):
            value = combine(cols_m, source[i])
            right_raw[base + i] = value
            split_store(split, base + i, value)
            return carry

        lax.fori_loop(0, BR // 2, step, 0, unroll=2)

    half(mine, core * 32)
    half(theirs, (1 - core) * 32)
    cols_0 = columns(mr0[:, 0:K])
    for i in range(BR):
        value = combine(cols_0, start[:, i * BLK : (i + 1) * BLK])
        right0[i] = value
        split_store(split0, i, value)
    out = pad_lanes(gram_of(split, split), gram_of(split, split0))
    multiply(scal, cols, rows, blocks, held, sems, split, acc, term_place, 16, True)
    for j in range(4):
        acc[j * 17 + 16] = out


def second_backward(
    scal, rows, cols, summed, ext, left_raw, ml1, blocks, own, other, left2_raw, left1, mr1, mh,
    held, sems, split, split1, acc, *, terms
):
    start_copies(blocks, held, sems)
    proj = ext[:, K : 2 * K] / terms
    inverse = inverse_factor(ext[:, 0:K] / terms - mmt(proj, proj))
    both = mm(inverse, proj)
    mr1[...] = pad_lanes(inverse)
    mh[...] = pad_lanes(both)
    cols_l = columns(ml1[:, 0:K])

    def left_step(i, carry):
        value = combine(cols_l, left_raw[i])
        left1[i] = value
        split_store(split1, i, value)
        return carry

    lax.fori_loop(0, BR, left_step, 0, unroll=2)
    cols_b = columns(both)

    def back_step(i, carry):
        left2_raw[i] = combine(cols_b, left_raw[i])
        return carry

    lax.fori_loop(0, BR, back_step, 0, unroll=2)
    cols_m = columns(inverse)

    def step(i, carry):
        value = combine(cols_m, summed[i]) - left2_raw[i]
        left2_raw[i] = value
        split_store(split, i, value)
        return carry

    lax.fori_loop(0, BR, step, 0, unroll=2)
    out = pad_lanes(gram_of(split, split), gram_of(split, split1))
    multiply(scal, rows, cols, blocks, held, sems, split, acc, doc_place(scal[1]), 8, False)
    for j in range(8):
        acc[j * 9 + 8] = out
    own[...] = acc[0:36]
    other[...] = acc[36:72]


def last_left(
    scal, mine, theirs, ext, left2_raw, left1, right_raw, right0, mr1, mh,
    left_out, right2_raw, right1, ext_out, split, split1, *, docs
):
    core = scal[1]
    proj = ext[:, K : 2 * K] / docs
    inverse = inverse_factor(ext[:, 0:K] / docs - mmt(proj, proj))
    both = mm(inverse, proj)
    cols_b = columns(both)
    for i in range(BR):
        left_out[:, i * BLK : (i + 1) * BLK] = combine(cols_b, left1[i])
    cols_r = columns(mh[:, 0:K])

    def right_step(i, carry):
        right1[i] = combine(cols_r, right0[i])
        right2_raw[i] = combine(cols_b, right_raw[i])
        return carry

    lax.fori_loop(0, BR, right_step, 0)
    cols_1 = columns(mr1[:, 0:K])

    def right1_step(i, carry):
        value = combine(cols_1, right_raw[i]) - right1[i]
        right1[i] = value
        split_store(split1, i, value)
        return carry

    lax.fori_loop(0, BR, right1_step, 0, unroll=2)
    cols_m = columns(inverse)

    def half(source, base):
        def step(i, carry):
            value = combine(cols_m, source[i]) - right2_raw[base + i]
            right2_raw[base + i] = value
            split_store(split, base + i, value)
            return carry

        lax.fori_loop(0, BR // 2, step, 0, unroll=2)

    half(mine, core * 32)
    half(theirs, (1 - core) * 32)
    for i in range(BR):
        part = slice(i * BLK, (i + 1) * BLK)
        left_out[:, part] = combine(cols_m, left2_raw[i]) - left_out[:, part]
    ext_out[...] = pad_lanes(gram_of(split, split), gram_of(split, split1))


def last_right(ext, right2_raw, right1, right_out, *, terms):
    proj = ext[:, K : 2 * K] / terms
    inverse = inverse_factor(ext[:, 0:K] / terms - mmt(proj, proj))
    cols_b = columns(mm(inverse, proj))
    for i in range(BR):
        right_out[:, i * BLK : (i + 1) * BLK] = combine(cols_b, right1[i])
    cols_m = columns(inverse)
    for i in range(BR):
        part = slice(i * BLK, (i + 1) * BLK)
        right_out[:, part] = combine(cols_m, right2_raw[i]) - right_out[:, part]


def panel(n=BR):
    return jax.ShapeDtypeStruct((n, K, BLK), F32)


SMALL = jax.ShapeDtypeStruct((K, BLK), F32)
WIDE = jax.ShapeDtypeStruct((K, BR * BLK), F32)
HELD = [VMEM((NB, BLK, BLK), BF), pltpu.SemaphoreType.DMA((NB // CHUNK,))]
SPLIT = VMEM((BR, 48, BLK), BF)


def call(body, name, args, outs, scratch, product=True):
    in_specs = []
    for i, a in enumerate(args):
        if product and i == len(args) - 1:
            in_specs.append(pl.BlockSpec(memory_space=pl.ANY))
        else:
            integer = a.dtype == jnp.int32
            in_specs.append(pl.BlockSpec(memory_space=SMEM if integer else VMEM))
    return pl.pallas_call(
        body,
        name=name,
        out_shape=outs,
        in_specs=in_specs,
        out_specs=jax.tree.map(lambda _: pl.BlockSpec(memory_space=VMEM), outs),
        scratch_shapes=scratch,
        compiler_params=pltpu.CompilerParams(vmem_limit_bytes=48 * 1024 * 1024),
    )(*args)


SWAP = [(0, 1), (1, 0)]


def copies(value):
    return jnp.broadcast_to(value[None], (4, *value.shape))


def sum_term(acc):
    parts = lax.all_to_all(acc.reshape(4, 17, K, BLK), "y", 0, 0)
    total = ((parts[0] + parts[1]) + parts[2]) + parts[3]
    total = total + lax.ppermute(total, "zh", SWAP)
    full = lax.all_to_all(copies(total[:16]), "y", 0, 0)
    return full.reshape(BR, K, BLK), total[16]


def sum_doc(own, other):
    total = own + lax.ppermute(other, "c", SWAP)
    for axis in ("x", "zl"):
        send = total.reshape(4, 9, K, BLK) if axis == "x" else copies(total)
        parts = lax.all_to_all(send, axis, 0, 0)
        total = ((parts[0] + parts[1]) + parts[2]) + parts[3]
    mine = lax.all_to_all(copies(total[:8]), "x", 0, 0).reshape(BR // 2, K, BLK)
    return mine, lax.ppermute(mine, "c", SWAP), total[8]


def local(blocks, block_rows, block_cols, counts, start):
    core = lax.axis_index("c").astype(jnp.int32)
    scal = jnp.stack([counts[0, 0], core])
    docs = float(BR * BLK * 32)
    terms = float(BR * BLK * 8)
    index = (scal, block_rows, block_cols)

    acc = call(first_forward, "first_forward", (*index, start, blocks), panel(68), [*HELD, SPLIT])
    summed, ext = sum_term(acc)
    own, other, left_raw, mr0 = call(
        functools.partial(first_backward, terms=terms),
        "first_backward",
        (*index, summed, ext, blocks),
        (panel(36), panel(36), panel(), SMALL),
        [*HELD, SPLIT, VMEM((72, K, BLK), F32)],
    )
    mine, theirs, ext = sum_doc(own, other)
    acc, right_raw, right0, ml1 = call(
        functools.partial(second_forward, docs=docs),
        "second_forward",
        (*index, mine, theirs, ext, start, mr0, blocks),
        (panel(68), panel(), panel(), SMALL),
        [*HELD, SPLIT, SPLIT],
    )
    summed, ext = sum_term(acc)
    own, other, left2_raw, left1, mr1, mh = call(
        functools.partial(second_backward, terms=terms),
        "second_backward",
        (*index, summed, ext, left_raw, ml1, blocks),
        (panel(36), panel(36), panel(), panel(), SMALL, SMALL),
        [*HELD, SPLIT, SPLIT, VMEM((72, K, BLK), F32)],
    )
    mine, theirs, ext = sum_doc(own, other)
    left_out, right2_raw, right1, ext = call(
        functools.partial(last_left, docs=docs),
        "last_left",
        (scal, mine, theirs, ext, left2_raw, left1, right_raw, right0, mr1, mh),
        (WIDE, panel(), panel(), SMALL),
        [SPLIT, SPLIT],
        product=False,
    )
    ext = jnp.sum(lax.all_to_all(jnp.broadcast_to(ext[None], (8, K, BLK)), TERM, 0, 0), axis=0)
    right_out = call(
        functools.partial(last_right, terms=terms),
        "last_right",
        (ext, right2_raw, right1),
        WIDE,
        [],
        product=False,
    )
    return left_out, right_out


def solution(mesh):
    fine = Mesh(
        np.asarray(mesh.devices).reshape(4, 4, 2, 4, 2), (*DOC, *TERM)
    )
    return jax.shard_map(
        local,
        mesh=fine,
        in_specs=(P(DOC, TERM, None, None), P(DOC, TERM), P(DOC, TERM), P(DOC, TERM), P(None, TERM)),
        out_specs=(P(None, DOC), P(None, TERM)),
        check_vma=False,
    )
```

time: 1210 us -> 247 us (0.20)
  waiting for transfers between devices: 757 us -> 24.2 us
  blocking collectives: 337 us -> 113 us
  matrix products: 58.6 us -> 0 us
  starting transfers between devices: 0.16 us -> 54 us
  Pallas kernels: 0 us -> 49.8 us
  other arithmetic: 21.7 us -> 0.41 us
  between operations: 14.8 us -> 1.49 us
    psum x4 -> x0, waiting for transfers between devices: 757 us -> none  [the longest x2 536 us: local(): summed_right = lax.psum(partial_right, 'doc')]
    psum x8 -> x0, blocking collectives: 337 us -> none  [the longest x3 212 us: left_reduce(): return lax.psum(values, 'doc')]
    all_to_all x0 -> x9, blocking collectives: none -> 113 us  [the longest x4 56.9 us: sum_doc(): parts = lax.all_to_all(send, axis, 0, 0)]
    dot_general x19 -> x0, matrix products: 53.6 us -> none  [the longest x4 27.7 us: slot_product(): jnp.einsum(pattern, tile_blocks, gathered, preferred_element_type=jnp.flo...]
    pallas_call x0 -> x6, Pallas kernels: none -> 49.8 us  [call(): pl.pallas_call(body, name=name, out_shape=outs, in_specs=in_specs, out_sp...]
    ppermute x0 -> x6, starting transfers between devices: none -> 47 us  [the longest x2 26.5 us: sum_doc(): total = own + lax.ppermute(other, 'c', SWAP)]
    another operation x25 -> x1, other arithmetic: 20 us -> 0.08 us  [local(): scal = jnp.stack([counts[0, 0], core])]
    all_to_all x0 -> x2, waiting for transfers between devices: none -> 13.9 us  [sum_term(): full = lax.all_to_all(copies(total[:16]), 'y', 0, 0)]
  transfers between devices with their start and end apart: 4 -> 8, of which waited for: 4 -> 8; matrix products, arithmetic and copies ran while one was open for 0% -> 0% of each run, Pallas kernels for 0% -> 0%
where the time goes in v1:
time: 247 us
  blocking collectives  113 us (46%)
  starting transfers between devices  54 us (22%)
  Pallas kernels  49.8 us (20%)
  waiting for transfers between devices  24.2 us (10%)
  local copies, waits for them, and re-layouts  4.22 us (2%)
    all_to_all x4, blocking collectives, sum_doc(): parts = lax.all_to_all(send, axis, 0, 0)  56.9 us
    pallas_call x6, Pallas kernels, call(): pl.pallas_call(body, name=name, out_shape=outs, in_specs=in_specs, out_sp...  49.8 us
    all_to_all x2, blocking collectives, sum_term(): parts = lax.all_to_all(acc.reshape(4, 17, K, BLK), 'y', 0, 0)  27 us
    ppermute x2, starting transfers between devices, sum_doc(): total = own + lax.ppermute(other, 'c', SWAP)  26.5 us
    all_to_all x2, blocking collectives, sum_doc(): mine = lax.all_to_all(copies(total[:8]), 'x', 0, 0).reshape(BR // 2, K, BLK)  15.8 us
    all_to_all x2, waiting for transfers between devices, sum_term(): full = lax.all_to_all(copies(total[:16]), 'y', 0, 0)  13.9 us
    all_to_all x1, blocking collectives, local(): lax.all_to_all(jnp.broadcast_to(ext[None], (8, K, BLK)), TERM, 0, 0)  13.5 us
    ppermute x2, starting transfers between devices, sum_term(): total = total + lax.ppermute(total, 'zh', SWAP)  12 us
  transfers between devices with their start and end apart: 8, of which 8 were waited for; matrix products, arithmetic and copies ran while one was open for 0% of the time, Pallas kernels for 0%

profile of v1, /device:TPU:1, one launch (start us, length us, event | category | flops | bytes accessed | tf_op | source)
XLA Modules:
  0.0 247.3 jit_solution(15723924163700002433)
XLA Ops:
  0.6 0.0 copy-start.5
  0.6 0.0 copy-start.3
  1.3 0.1 pad_add_fusion.scal
  1.4 0.0 copy-start
  1.4 1.0 copy-done
  2.4 0.0 copy-start.2
  2.4 0.7 copy-done.2
  3.1 0.0 copy-start.4
  3.1 0.7 copy-done.4
  3.8 5.6 %first_forward.1 = f32[68,16,128]{2,1,0:T(8,128)S(1)} custom-call(s32[2]{0:T(128)S(1)} %pad_add_fusion.scal, s32[1,320]{1,0:T(1,128)S(1)} %copy-done.2, s32[1,320]{1,0:T(1,128)S(1)} %copy-done.4, f32[16,8192]{1,0:T(8,128)S(1)} %copy-done, bf16[1,320,128,128]{3,2,1,0:T(8,128)(2,1)} %blocks.7), custom_call_target="tpu_custom_call" | custom-call | tf_op jit(solution)/shard_map/first_forward/pallas_call | solution.py:323
  9.4 0.0 copy-start.1
  9.4 14.8 %all_to_all.55 = f32[4,17,16,128]{3,2,1,0:T(8,128)S(1)} all-to-all(f32[4,17,16,128]{3,2,1,0:T(8,128)S(1)} %bitcast.35), channel_id=1, replica_groups=mesh['zl'=4,'x'=4,'c'=2,'y'=4,'zh'=2] {'y'}, dimensions={0} | all-to-all | bytes 1114112 | tf_op jit(solution)/shard_map/all_to_all | solution.py:342
  24.2 7.2 %collective-permute-start = (f32[17,16,128]{2,1,0:T(8,128)S(1)}, f32[17,16,128]{2,1,0:T(8,128)S(1)}, u32[]{:S(2)}, u32[]{:S(2)}) collective-permute-start(f32[17,16,128]{2,1,0:T(8,128)S(1)} %fusion.1), channel_id=1, source_target_pairs={{0,1},{1,0},{2,3},{3,2},{4,5},{5,4},{6,7},{7,6},{8,9},{9,8},{10,11... | collective-permute-start | bytes 417800 | tf_op jit(solution)/shard_map/ppermute | solution.py:344
  31.4 2.4 collective-permute-done
  33.8 0.1 fusion.5
  33.9 0.8 broadcast_in_dim.18
  34.7 3.5 %all-to-all-start.1 = ((f32[4,16,16,128]{3,2,1,0:T(8,128)}), f32[4,16,16,128]{3,2,1,0:T(8,128)S(1)}, u32[]{:S(2)}, u32[]{:S(2)}) async-start(f32[4,16,16,128]{3,2,1,0:T(8,128)} %broadcast_in_dim.18), calls=%async_computation.1 | async-start | bytes 1048576 | tf_op jit(solution)/shard_map/all_to_all | solution.py:345
  38.2 7.0 %all-to-all-done.1 = f32[4,16,16,128]{3,2,1,0:T(8,128)S(1)} async-done(((f32[4,16,16,128]{3,2,1,0:T(8,128)}), f32[4,16,16,128]{3,2,1,0:T(8,128)S(1)}, u32[]{:S(2)}, u32[]{:S(2)}) %all-to-all-start.1) | async-done | bytes 524320 | tf_op jit(solution)/shard_map/all_to_all | solution.py:345
  45.2 0.0 copy-done.5
  45.3 0.0 copy-done.3
  45.3 7.1 %first_backward.1 = (f32[36,16,128]{2,1,0:T(8,128)S(1)}, f32[36,16,128]{2,1,0:T(8,128)S(1)}, f32[64,16,128]{2,1,0:T(8,128)S(1)}, f32[16,128]{1,0:T(8,128)S(1)}) custom-call(s32[2]{0:T(128)S(1)} %pad_add_fusion.scal, s32[1,320]{1,0:T(1,128)S(1)} %copy-done.3, s32[1,320]{1,0:T(1,128)S(1)} %copy-done.5, f32[64,16,128]{2,1,0:T(8,128)S(1)} %bitcast.37, ...), custom_call_target="tpu_custom_call" | custom-call | tf_op jit(solution)/shard_map/first_backward/pallas_call | solution.py:323
  52.4 13.8 %collective-permute-start.1 = (f32[36,16,128]{2,1,0:T(8,128)S(1)}, f32[36,16,128]{2,1,0:T(8,128)S(1)}, u32[]{:S(2)}, u32[]{:S(2)}) collective-permute-start(f32[36,16,128]{2,1,0:T(8,128)S(1)} %get-tuple-element.21), channel_id=1, source_target_pairs={{0,8},{8,0},{1,9},{9,1},{2,10},{10,2},{3,11},{11,3},{4,12},{12,4},... | collective-permute-start | bytes 884744 | tf_op jit(solution)/shard_map/ppermute | solution.py:350
  66.2 1.2 collective-permute-done.1
  67.4 14.6 %all_to_all.56 = f32[4,9,16,128]{3,2,1,0:T(8,128)S(1)} all-to-all(f32[4,9,16,128]{3,2,1,0:T(8,128)S(1)} %bitcast.43), channel_id=1, replica_groups=mesh['zl'=4,'x'=4,'c'=2,'y'=4,'zh'=2] {'x'}, dimensions={0} | all-to-all | bytes 589824 | tf_op jit(solution)/shard_map/all_to_all | solution.py:353
  82.1 13.2 %all_to_all.57 = f32[4,9,16,128]{3,2,1,0:T(8,128)S(1)} all-to-all(f32[4,9,16,128]{3,2,1,0:T(8,128)S(1)} %broadcast_in_dim.20), channel_id=1, replica_groups=mesh['zl'=4,'x'=4,'c'=2,'y'=4,'zh'=2] {'zl'}, dimensions={0} | all-to-all | bytes 589824 | tf_op jit(solution)/shard_map/all_to_all | solution.py:353
  95.4 7.9 %all_to_all.58 = f32[4,8,16,128]{3,2,1,0:T(8,128)S(1)} all-to-all(f32[4,8,16,128]{3,2,1,0:T(8,128)S(1)} %broadcast_in_dim.21), channel_id=1, replica_groups=mesh['zl'=4,'x'=4,'c'=2,'y'=4,'zh'=2] {'x'}, dimensions={0} | all-to-all | bytes 524288 | tf_op jit(solution)/shard_map/all_to_all | solution.py:355
  103.3 4.2 %collective-permute-start.2 = (f32[32,16,128]{2,1,0:T(8,128)S(1)}, f32[32,16,128]{2,1,0:T(8,128)S(1)}, u32[]{:S(2)}, u32[]{:S(2)}) collective-permute-start(f32[32,16,128]{2,1,0:T(8,128)S(1)} %bitcast.40), channel_id=1, source_target_pairs={{0,8},{8,0},{1,9},{9,1},{2,10},{10,2},{3,11},{11,3},{4,12},{12,4},... | collective-permute-start | bytes 786440 | tf_op jit(solution)/shard_map/ppermute | solution.py:356
  107.5 1.2 collective-permute-done.2.theirs
  108.7 0.0 copy-done.1
  108.7 10.2 %second_forward.1 = (f32[68,16,128]{2,1,0:T(8,128)S(1)}, f32[64,16,128]{2,1,0:T(8,128)S(1)}, f32[64,16,128]{2,1,0:T(8,128)S(1)}, f32[16,128]{1,0:T(8,128)S(1)}) custom-call(s32[2]{0:T(128)S(1)} %pad_add_fusion.scal, s32[1,320]{1,0:T(1,128)S(1)} %copy-done.3, s32[1,320]{1,0:T(1,128)S(1)} %copy-done.5, f32[32,16,128]{2,1,0:T(8,128)S(1)} %bitcast.41, ...), custom_call_target="tpu_custom_call" | custom-call | tf_op jit(solution)/shard_map/second_forward/pallas_call | solution.py:323
  118.9 12.2 %all_to_all.59 = f32[4,17,16,128]{3,2,1,0:T(8,128)S(1)} all-to-all(f32[4,17,16,128]{3,2,1,0:T(8,128)S(1)} %bitcast.42), channel_id=1, replica_groups=mesh['zl'=4,'x'=4,'c'=2,'y'=4,'zh'=2] {'y'}, dimensions={0} | all-to-all | bytes 1114112 | tf_op jit(solution)/shard_map/all_to_all | solution.py:342
  131.1 4.8 %collective-permute-start.3 = (f32[17,16,128]{2,1,0:T(8,128)S(1)}, f32[17,16,128]{2,1,0:T(8,128)S(1)}, u32[]{:S(2)}, u32[]{:S(2)}) collective-permute-start(f32[17,16,128]{2,1,0:T(8,128)S(1)} %fusion), channel_id=1, source_target_pairs={{0,1},{1,0},{2,3},{3,2},{4,5},{5,4},{6,7},{7,6},{8,9},{9,8},{10,11... | collective-permute-start | bytes 417800 | tf_op jit(solution)/shard_map/ppermute | solution.py:344
  135.9 3.1 %collective-permute-done.3 = f32[17,16,128]{2,1,0:T(8,128)S(1)} collective-permute-done((f32[17,16,128]{2,1,0:T(8,128)S(1)}, f32[17,16,128]{2,1,0:T(8,128)S(1)}, u32[]{:S(2)}, u32[]{:S(2)}) %collective-permute-start.3) | collective-permute-done | bytes 139296 | tf_op jit(solution)/shard_map/ppermute | solution.py:344
  139.0 0.8 broadcast_in_dim.22
  139.9 3.5 %all-to-all-start.6 = ((f32[4,16,16,128]{3,2,1,0:T(8,128)}), f32[4,16,16,128]{3,2,1,0:T(8,128)S(1)}, u32[]{:S(2)}, u32[]{:S(2)}) async-start(f32[4,16,16,128]{3,2,1,0:T(8,128)} %broadcast_in_dim.22), calls=%async_computation.6 | async-start | bytes 1048576 | tf_op jit(solution)/shard_map/all_to_all | solution.py:345
  143.4 6.9 %all-to-all-done.6 = f32[4,16,16,128]{3,2,1,0:T(8,128)S(1)} async-done(((f32[4,16,16,128]{3,2,1,0:T(8,128)}), f32[4,16,16,128]{3,2,1,0:T(8,128)S(1)}, u32[]{:S(2)}, u32[]{:S(2)}) %all-to-all-start.6) | async-done | bytes 524320 | tf_op jit(solution)/shard_map/all_to_all | solution.py:345
  150.3 11.2 %second_backward.1 = (f32[36,16,128]{2,1,0:T(8,128)S(1)}, f32[36,16,128]{2,1,0:T(8,128)S(1)}, f32[64,16,128]{2,1,0:T(8,128)S(1)}, f32[64,16,128]{2,1,0:T(8,128)S...) custom-call(s32[2]{0:T(128)S(1)} %pad_add_fusion.scal, s32[1,320]{1,0:T(1,128)S(1)} %copy-done.3, ...), custom_call_target="tpu_custom_call" | custom-call | tf_op jit(solution)/shard_map/second_backward/pallas_call | solution.py:323
  161.5 12.7 %collective-permute-start.4 = (f32[36,16,128]{2,1,0:T(8,128)S(1)}, f32[36,16,128]{2,1,0:T(8,128)S(1)}, u32[]{:S(2)}, u32[]{:S(2)}) collective-permute-start(f32[36,16,128]{2,1,0:T(8,128)S(1)} %get-tuple-element.27), channel_id=1, source_target_pairs={{0,8},{8,0},{1,9},{9,1},{2,10},{10,2},{3,11},{11,3},{4,12},{12,4},... | collective-permute-start | bytes 884744 | tf_op jit(solution)/shard_map/ppermute | solution.py:350
  174.2 1.2 collective-permute-done.4
  175.5 19.3 %all_to_all.60 = f32[4,9,16,128]{3,2,1,0:T(8,128)S(1)} all-to-all(f32[4,9,16,128]{3,2,1,0:T(8,128)S(1)} %bitcast.44), channel_id=1, replica_groups=mesh['zl'=4,'x'=4,'c'=2,'y'=4,'zh'=2] {'x'}, dimensions={0} | all-to-all | bytes 589824 | tf_op jit(solution)/shard_map/all_to_all | solution.py:353
  194.8 9.8 %all_to_all.61 = f32[4,9,16,128]{3,2,1,0:T(8,128)S(1)} all-to-all(f32[4,9,16,128]{3,2,1,0:T(8,128)S(1)} %broadcast_in_dim.24), channel_id=1, replica_groups=mesh['zl'=4,'x'=4,'c'=2,'y'=4,'zh'=2] {'zl'}, dimensions={0} | all-to-all | bytes 589824 | tf_op jit(solution)/shard_map/all_to_all | solution.py:353
  204.7 7.9 %all_to_all.62 = f32[4,8,16,128]{3,2,1,0:T(8,128)S(1)} all-to-all(f32[4,8,16,128]{3,2,1,0:T(8,128)S(1)} %broadcast_in_dim.25), channel_id=1, replica_groups=mesh['zl'=4,'x'=4,'c'=2,'y'=4,'zh'=2] {'x'}, dimensions={0} | all-to-all | bytes 524288 | tf_op jit(solution)/shard_map/all_to_all | solution.py:355
  212.6 4.2 %collective-permute-start.5 = (f32[32,16,128]{2,1,0:T(8,128)S(1)}, f32[32,16,128]{2,1,0:T(8,128)S(1)}, u32[]{:S(2)}, u32[]{:S(2)}) collective-permute-start(f32[32,16,128]{2,1,0:T(8,128)S(1)} %bitcast.38), channel_id=1, source_target_pairs={{0,8},{8,0},{1,9},{9,1},{2,10},{10,2},{3,11},{11,3},{4,12},{12,4},... | collective-permute-start | bytes 786440 | tf_op jit(solution)/shard_map/ppermute | solution.py:356
  216.9 1.2 collective-permute-done.5.theirs
  218.0 11.7 %last_left.1 = (f32[16,8192]{1,0:T(8,128)}, f32[64,16,128]{2,1,0:T(8,128)S(1)}, f32[64,16,128]{2,1,0:T(8,128)S(1)}, f32[16,128]{1,0:T(8,128)S(1)}) custom-call(s32[2]{0:T(128)S(1)} %pad_add_fusion.scal, f32[32,16,128]{2,1,0:T(8,128)S(1)} %bitcast.39, f32[32,16,128]{2,1,0:T(8,128)S(1)} %collective-permute-done.5.theirs, ...), custom_call_target="tpu_custom_call" | custom-call | tf_op jit(solution)/shard_map/last_left/pallas_call | solution.py:323
  229.7 13.5 %all_to_all.63 = f32[8,16,128]{2,1,0:T(8,128)S(1)} all-to-all(f32[8,16,128]{2,1,0:T(8,128)S(1)} %broadcast_in_dim.26), channel_id=1, replica_groups=mesh['zl'=4,'x'=4,'c'=2,'y'=4,'zh'=2] {'y','zh'}, dimensions={0} | all-to-all | bytes 131072 | tf_op jit(solution)/shard_map/all_to_all | solution.py:400
  243.3 4.0 %last_right.1 = f32[16,8192]{1,0:T(8,128)} custom-call(f32[16,128]{1,0:T(8,128)S(1)} %reduce_sum.9.ext, f32[64,16,128]{2,1,0:T(8,128)S(1)} %get-tuple-element.36.right2_raw, f32[64,16,128]{2,1,0:T(8,128)S(1)} %get-tuple-element.37.right1), custom_call_target="tpu_custom_call" | custom-call | tf_op jit(solution)/shard_map/last_right/pallas_call | solution.py:323
  (23 shorter events, 0.4 us)
Async XLA Ops:
  0.6 44.6 %copy-start.5 = (s32[1,320]{1,0:T(1,128)S(1)}, s32[1,320]{1,0:T(1,128)}, u32[]{:S(2)}) copy-start(s32[1,320]{1,0:T(1,128)} %cols.7) | copy-start | bytes 3844
  0.6 44.6 %copy-start.3 = (s32[1,320]{1,0:T(1,128)S(1)}, s32[1,320]{1,0:T(1,128)}, u32[]{:S(2)}) copy-start(s32[1,320]{1,0:T(1,128)} %rows.7) | copy-start | bytes 3844
  1.4 1.0 copy-start
  2.4 0.7 copy-start.2
  3.1 0.7 copy-start.4
  9.4 99.3 %copy-start.1 = (f32[16,8192]{1,0:T(8,128)S(1)}, f32[16,8192]{1,0:T(8,128)}, u32[]{:S(2)}) copy-start(f32[16,8192]{1,0:T(8,128)} %start.3) | copy-start | bytes 1572868
  24.2 9.6 %collective-permute-start = (f32[17,16,128]{2,1,0:T(8,128)S(1)}, f32[17,16,128]{2,1,0:T(8,128)S(1)}, u32[]{:S(2)}, u32[]{:S(2)}) collective-permute-start(f32[17,16,128]{2,1,0:T(8,128)S(1)} %fusion.1), channel_id=1, source_target_pairs={{0,1},{1,0},{2,3},{3,2},{4,5},{5,4},{6,7},{7,6},{8,9},{9,8},{10,11... | collective-permute-start | bytes 417800 | tf_op jit(solution)/shard_map/ppermute | solution.py:344
  34.7 10.5 %all-to-all-start.1 = ((f32[4,16,16,128]{3,2,1,0:T(8,128)}), f32[4,16,16,128]{3,2,1,0:T(8,128)S(1)}, u32[]{:S(2)}, u32[]{:S(2)}) async-start(f32[4,16,16,128]{3,2,1,0:T(8,128)} %broadcast_in_dim.18), calls=%async_computation.1 | async-start | bytes 1048576 | tf_op jit(solution)/shard_map/all_to_all | solution.py:345
  52.4 15.0 %collective-permute-start.1 = (f32[36,16,128]{2,1,0:T(8,128)S(1)}, f32[36,16,128]{2,1,0:T(8,128)S(1)}, u32[]{:S(2)}, u32[]{:S(2)}) collective-permute-start(f32[36,16,128]{2,1,0:T(8,128)S(1)} %get-tuple-element.21), channel_id=1, source_target_pairs={{0,8},{8,0},{1,9},{9,1},{2,10},{10,2},{3,11},{11,3},{4,12},{12,4},... | collective-permute-start | bytes 884744 | tf_op jit(solution)/shard_map/ppermute | solution.py:350
  103.3 5.4 %collective-permute-start.2 = (f32[32,16,128]{2,1,0:T(8,128)S(1)}, f32[32,16,128]{2,1,0:T(8,128)S(1)}, u32[]{:S(2)}, u32[]{:S(2)}) collective-permute-start(f32[32,16,128]{2,1,0:T(8,128)S(1)} %bitcast.40), channel_id=1, source_target_pairs={{0,8},{8,0},{1,9},{9,1},{2,10},{10,2},{3,11},{11,3},{4,12},{12,4},... | collective-permute-start | bytes 786440 | tf_op jit(solution)/shard_map/ppermute | solution.py:356
  131.1 7.9 %collective-permute-start.3 = (f32[17,16,128]{2,1,0:T(8,128)S(1)}, f32[17,16,128]{2,1,0:T(8,128)S(1)}, u32[]{:S(2)}, u32[]{:S(2)}) collective-permute-start(f32[17,16,128]{2,1,0:T(8,128)S(1)} %fusion), channel_id=1, source_target_pairs={{0,1},{1,0},{2,3},{3,2},{4,5},{5,4},{6,7},{7,6},{8,9},{9,8},{10,11... | collective-permute-start | bytes 417800 | tf_op jit(solution)/shard_map/ppermute | solution.py:344
  139.9 10.4 %all-to-all-start.6 = ((f32[4,16,16,128]{3,2,1,0:T(8,128)}), f32[4,16,16,128]{3,2,1,0:T(8,128)S(1)}, u32[]{:S(2)}, u32[]{:S(2)}) async-start(f32[4,16,16,128]{3,2,1,0:T(8,128)} %broadcast_in_dim.22), calls=%async_computation.6 | async-start | bytes 1048576 | tf_op jit(solution)/shard_map/all_to_all | solution.py:345
  161.5 13.9 %collective-permute-start.4 = (f32[36,16,128]{2,1,0:T(8,128)S(1)}, f32[36,16,128]{2,1,0:T(8,128)S(1)}, u32[]{:S(2)}, u32[]{:S(2)}) collective-permute-start(f32[36,16,128]{2,1,0:T(8,128)S(1)} %get-tuple-element.27), channel_id=1, source_target_pairs={{0,8},{8,0},{1,9},{9,1},{2,10},{10,2},{3,11},{11,3},{4,12},{12,4},... | collective-permute-start | bytes 884744 | tf_op jit(solution)/shard_map/ppermute | solution.py:350
  212.6 5.4 %collective-permute-start.5 = (f32[32,16,128]{2,1,0:T(8,128)S(1)}, f32[32,16,128]{2,1,0:T(8,128)S(1)}, u32[]{:S(2)}, u32[]{:S(2)}) collective-permute-start(f32[32,16,128]{2,1,0:T(8,128)S(1)} %bitcast.38), channel_id=1, source_target_pairs={{0,8},{8,0},{1,9},{9,1},{2,10},{10,2},{3,11},{11,3},{4,12},{12,4},... | collective-permute-start | bytes 786440 | tf_op jit(solution)/shard_map/ppermute | solution.py:356
